TPU v7x, 256 devices: a whole 4x4x8 slice. The times are simulated.
256 devices in a mesh: fsdp: 64 (over z, x, core), rep: 4 (over y).
Axes of the slice: x: 4, y: 4, z: 8, core: 2. Of those that a mesh axis runs over, the one named last changes fastest.
Arguments:
- replica_grads: bfloat16 [4, 2048, 18944], P('rep', 'fsdp'), may hold values from -2 to 2
- block_owner: int32 [4, 37], replicated, may hold values from 0 to 63, as said below
- left_factor: float32 [64, 4, 1, 512, 512], P('fsdp', 'rep'), may hold values from -1 to 21, as said below
- right_factor: float32 [64, 4, 1, 512, 512], P('fsdp', 'rep'), may hold values from -1 to 21, as said below
- left_root: bfloat16 [64, 4, 1, 512, 512], P('fsdp', 'rep'), may hold values from -1 to 3, as said below
- right_root: bfloat16 [64, 4, 1, 512, 512], P('fsdp', 'rep'), may hold values from -1 to 3, as said below
- moment: float32 [64, 4, 1, 512, 512], P('fsdp', 'rep'), may hold values from 1e-05 to 0.01
Outputs:
- direction: bfloat16 [2048, 18944], P('fsdp')
- left_new: float32 [64, 4, 1, 512, 512], P('fsdp', 'rep')
- right_new: float32 [64, 4, 1, 512, 512], P('fsdp', 'rep')
- moment_new: float32 [64, 4, 1, 512, 512], P('fsdp', 'rep')
Inputs may be any that keep to these rules, and one draw needn't show every extreme that they name: `block_owner`: within each of the 4 block rows no owner holds more than 1 of the 37 blocks, and some owner holds exactly 1. `left_factor`: Symmetric. `right_factor`: Symmetric. `left_root`: Symmetric. `right_root`: Symmetric.
All inputs are finite; a program needn't handle non-finite values.
Results may differ from a plain program's by a relative error of at most 0.017.
Values may be sent and summed in bfloat16 or wider, within the bound.
A program may use at most 128 MiB of HBM per device.

v0:
```python
import jax
import jax.numpy as jnp
from jax import lax
from jax.sharding import PartitionSpec as P

stat_decay = 0.9
graft_decay = 0.99
adam_epsilon = 1e-08
graft_epsilon = 1e-06


def slot_ranks(block_owner):
    columns = jnp.arange(block_owner.shape[1], dtype=jnp.int32)
    earlier = (block_owner[:, :, None] == block_owner[:, None, :]) & (
        columns[None, None, :] < columns[None, :, None]
    )
    return jnp.sum(earlier.astype(jnp.int32), axis=2)


def precondition(gradient, left_old, right_old, left_root, right_root, moment_old):
    highest = lax.Precision.HIGHEST
    left_new = stat_decay * left_old + (1.0 - stat_decay) * jnp.einsum(
        "sij,skj->sik", gradient, gradient, precision=highest
    )
    right_new = stat_decay * right_old + (1.0 - stat_decay) * jnp.einsum(
        "sji,sjk->sik", gradient, gradient, precision=highest
    )
    moment_new = graft_decay * moment_old + (1.0 - graft_decay) * gradient * gradient
    adam_step = gradient / (jnp.sqrt(moment_new) + adam_epsilon)
    low_grad = gradient.astype(jnp.bfloat16)
    half_done = jnp.einsum(
        "sij,sjk->sik", left_root, low_grad, preferred_element_type=jnp.float32
    ).astype(jnp.bfloat16)
    conditioned = jnp.einsum(
        "sij,sjk->sik", half_done, right_root, preferred_element_type=jnp.float32
    )
    graft_scale = jnp.sqrt(
        (jnp.mean(adam_step * adam_step, axis=(1, 2)) + graft_epsilon)
        / (jnp.mean(conditioned * conditioned, axis=(1, 2)) + graft_epsilon)
    )
    step_blocks = (graft_scale[:, None, None] * conditioned).astype(jnp.bfloat16)
    return (left_new, right_new, moment_new, step_blocks)


def local(replica_grads, block_owner, left_factor, right_factor, left_root, right_root, moment):
    owner_count = lax.axis_size("fsdp")
    shard_grad = replica_grads[0]
    shard_rows = shard_grad.shape[0]
    full_width = shard_grad.shape[1]
    slot_count = left_factor.shape[2]
    block_size = left_factor.shape[4]
    columns = full_width // block_size
    per_row = block_size // shard_rows
    shard_index = lax.axis_index("fsdp")
    replica_index = lax.axis_index("rep")
    home_row = shard_index // per_row
    slot_rank = slot_ranks(block_owner)
    row_owner = lax.dynamic_index_in_dim(block_owner, home_row, 0, keepdims=False)
    row_slot = lax.dynamic_index_in_dim(slot_rank, home_row, 0, keepdims=False)
    target = row_slot * owner_count + row_owner
    routing = target[None, :] == jnp.arange(slot_count * owner_count, dtype=jnp.int32)[:, None]
    send_shape = (slot_count, owner_count, shard_rows, block_size)
    block_shape = (slot_count, block_size, block_size)
    summed = lax.psum(shard_grad.astype(jnp.float32).astype(jnp.bfloat16), "rep").astype(
        jnp.float32
    )
    outbound = jnp.einsum(
        "pc,rcb->prb",
        routing.astype(jnp.float32),
        summed.reshape(shard_rows, columns, block_size),
        precision=lax.Precision.HIGHEST,
    )
    landed = lax.all_to_all(
        outbound.reshape(send_shape).astype(jnp.bfloat16),
        "fsdp",
        split_axis=1,
        concat_axis=1,
        tiled=True,
    ).astype(jnp.float32)
    my_rows = lax.dynamic_slice_in_dim(landed, replica_index * per_row, per_row, 1)
    gradient = my_rows.reshape(block_shape)
    left_new, right_new, moment_new, step_blocks = precondition(
        gradient,
        left_factor.reshape(block_shape),
        right_factor.reshape(block_shape),
        left_root.reshape(block_shape),
        right_root.reshape(block_shape),
        moment.reshape(block_shape),
    )
    picker = routing.T.astype(jnp.bfloat16)
    every_row = lax.all_gather(step_blocks[:, None], "rep", axis=1, tiled=True)
    arrived = lax.all_to_all(
        every_row.reshape(send_shape), "fsdp", split_axis=1, concat_axis=1, tiled=True
    )
    picked = jnp.einsum(
        "cp,prb->rcb",
        picker,
        arrived.reshape(slot_count * owner_count, shard_rows, block_size),
        preferred_element_type=jnp.float32,
    )
    direction = picked.astype(jnp.bfloat16).reshape(shard_rows, full_width)
    state_shape = left_factor.shape
    return (
        direction,
        left_new.reshape(state_shape),
        right_new.reshape(state_shape),
        moment_new.reshape(state_shape),
    )


def solution(mesh):
    return jax.shard_map(
        local,
        mesh=mesh,
        in_specs=(
            P("rep", "fsdp", None),
            P(),
            P("fsdp", "rep", None, None, None),
            P("fsdp", "rep", None, None, None),
            P("fsdp", "rep", None, None, None),
            P("fsdp", "rep", None, None, None),
            P("fsdp", "rep", None, None, None),
        ),
        out_specs=(
            P("fsdp", None),
            P("fsdp", "rep", None, None, None),
            P("fsdp", "rep", None, None, None),
            P("fsdp", "rep", None, None, None),
        ),
        check_vma=False,
    )
```

profile of v0, /device:TPU:32, one launch (start us, length us, event | category | flops | bytes accessed | tf_op | source)
XLA Modules:
  0.0 238.7 jit_solution(12591702448274841129)
XLA Ops:
  7.2 0.0 copy-start
  7.2 0.0 copy-start.3
  7.2 0.0 all-reduce.2.cloned.1.call-start
  7.2 2.7 %reshape.174 = bf16[32,37,512]{2,1,0:T(8,128)(2,1)} reshape(bf16[1,32,18944]{2,1,0:T(8,128)(2,1)} %param.7) | data formatting | bytes 2424832 | tf_op jit(solution)/shard_map/reshape | solution.py:70
  9.9 0.0 all-reduce.2.cloned.1.call-update
  10.0 0.0 copy-done.3
  10.0 0.1 copy.30
  10.1 0.8 convert_reduce_fusion
  10.9 0.2 add_reduce_fusion
  11.0 55.0 %all-reduce.2.cloned.1.call-done = bf16[32,37,512]{2,1,0:T(8,128)(2,1)} async-done(((bf16[32,37,512]{2,1,0:T(8,128)(2,1)}), bf16[32,37,512]{2,1,0:T(8,128)(2,1)}) %all-reduce.2.cloned.1.call-update) | async-done | bytes 1212432 | tf_op jit(solution)/shard_map/psum | solution.py:64
  66.0 2.1 convert_bitcast_fusion
  68.2 2.5 %copy.32 = bf16[1,64,32,512]{3,2,0,1:T(8,128)(2,1)} copy(bf16[1,64,32,512]{3,1,2,0:T(8,128)(2,1)S(1)} %convert_bitcast_fusion) | data formatting | bytes 4194304 | tf_op jit(solution)/shard_map/convert_element_type | solution.py:74
  70.7 0.0 copy-start.1
  70.7 10.8 %all-to-all-start = ((bf16[1,64,32,512]{3,2,0,1:T(8,128)(2,1)}), bf16[1,64,32,512]{3,2,0,1:T(8,128)(2,1)}, u32[]{:S(2)}, u32[]{:S(2)}) async-start(bf16[1,64,32,512]{3,2,0,1:T(8,128)(2,1)} %copy.32), calls=%async_computation | async-start | bytes 4194304 | tf_op jit(solution)/shard_map/all_to_all | solution.py:73
  81.4 0.0 all-gather.3.cloned.1.call-start
  81.5 0.0 copy-done.1
  81.5 0.1 broadcast_multiply_fusion
  81.6 0.0 copy-start.5
  81.6 50.1 %all-to-all-done = bf16[1,64,32,512]{3,2,0,1:T(8,128)(2,1)} async-done(((bf16[1,64,32,512]{3,2,0,1:T(8,128)(2,1)}), bf16[1,64,32,512]{3,2,0,1:T(8,128)(2,1)}, u32[]{:S(2)}, u32[]{:S(2)}) %all-to-all-start) | async-done | bytes 2097184 | tf_op jit(solution)/shard_map/all_to_all | solution.py:73
  131.8 2.2 fusion.18
  134.0 0.0 copy-done
  134.0 0.0 copy-done.5
  134.1 1.6 multiply_reduce_fusion
  137.0 0.9 multiply_convert_fusion
  137.9 0.0 all-gather.3.cloned.1.call-update
  138.0 30.0 %all-gather.3.cloned.1.call-done = bf16[2048,512]{1,0:T(8,128)(2,1)} async-done(((bf16[512,512]{1,0:T(8,128)(2,1)}), bf16[2048,512]{1,0:T(8,128)(2,1)}) %all-gather.3.cloned.1.call-update) | async-done | bytes 2097168 | tf_op jit(solution)/shard_map/all_gather | solution.py:91
  168.0 10.5 %all-to-all-start.1 = ((bf16[1,64,32,512]{3,2,0,1:T(8,128)(2,1)}), bf16[1,64,32,512]{3,2,0,1:T(8,128)(2,1)S(1)}, u32[]{:S(2)}, u32[]{:S(2)}) async-start(bf16[1,64,32,512]{3,2,0,1:T(8,128)(2,1)} %bitcast.62), calls=%async_computation.1 | async-start | bytes 4194304 | tf_op jit(solution)/shard_map/all_to_all | solution.py:92
  178.4 0.0 copy-start.2
  178.4 2.8 %fusion.8 = f32[1,1,1,512,512]{4,3,2,1,0:T(8,128)} fusion(bf16[512,512]{1,0:T(8,128)(2,1)S(1)} %bitcast.58, f32[1,1,1,512,512]{4,3,2,1,0:T(8,128)} %param.9), kind=kOutput, calls=%fused_computation.11 | convolution fusion | flops 269221888 | bytes 2621440 | tf_op jit(solution)/shard_map/sij,skj->sik/dot_general | solution.py:22
  181.2 0.0 copy-start.4
  181.2 0.0 copy-done.2
  181.2 1.2 fusion.17
  182.4 0.3 copy-done.4
  182.7 1.4 fusion.10
  184.2 44.7 %all-to-all-done.1 = bf16[1,64,32,512]{3,2,0,1:T(8,128)(2,1)S(1)} async-done(((bf16[1,64,32,512]{3,2,0,1:T(8,128)(2,1)}), bf16[1,64,32,512]{3,2,0,1:T(8,128)(2,1)S(1)}, u32[]{:S(2)}, u32[]{:S(2)}) %all-to-all-start.1) | async-done | bytes 2097184 | tf_op jit(solution)/shard_map/all_to_all | solution.py:92
  228.8 1.6 fusion.3
  230.4 1.4 copy.37
  (2 shorter events, 0.0 us)
Async XLA Ops:
  7.2 126.9 %copy-start = (bf16[1,1,1,512,512]{4,3,2,1,0:T(8,128)(2,1)S(1)}, bf16[1,1,1,512,512]{4,3,2,1,0:T(8,128)(2,1)}, u32[]{:S(2)}) copy-start(bf16[1,1,1,512,512]{4,3,2,1,0:T(8,128)(2,1)} %param.12) | copy-start | bytes 1572868
  7.2 2.8 %copy-start.3 = (s32[4,37]{1,0:T(4,128)S(1)}, s32[4,37]{1,0:T(4,128)}, u32[]{:S(2)}) copy-start(s32[4,37]{1,0:T(4,128)} %param.8) | copy-start | bytes 1780
  7.2 58.8 %all-reduce.2.cloned.1.call-start = ((), (), s32[]{:S(2)}) async-start(), calls=%async_computation.2 | async-start | bytes 2621440 | tf_op jit(solution)/shard_map/psum | solution.py:64
  70.7 10.8 %copy-start.1 = (f32[1,1,1,512,512]{4,3,2,1,0:T(8,128)S(1)}, f32[1,1,1,512,512]{4,3,2,1,0:T(8,128)}, u32[]{:S(2)}) copy-start(f32[1,1,1,512,512]{4,3,2,1,0:T(8,128)} %param.13) | copy-start | bytes 3145732
  70.7 61.1 %all-to-all-start = ((bf16[1,64,32,512]{3,2,0,1:T(8,128)(2,1)}), bf16[1,64,32,512]{3,2,0,1:T(8,128)(2,1)}, u32[]{:S(2)}, u32[]{:S(2)}) async-start(bf16[1,64,32,512]{3,2,0,1:T(8,128)(2,1)} %copy.32), calls=%async_computation | async-start | bytes 4194304 | tf_op jit(solution)/shard_map/all_to_all | solution.py:73
  81.4 86.5 %all-gather.3.cloned.1.call-start = ((), (), s32[]{:S(2)}) async-start(), calls=%async_computation.3 | async-start | bytes 2621440 | tf_op jit(solution)/shard_map/all_gather | solution.py:91
  81.6 52.4 %copy-start.5 = (bf16[1,1,1,512,512]{4,3,2,1,0:T(8,128)(2,1)S(1)}, bf16[1,1,1,512,512]{4,3,2,1,0:T(8,128)(2,1)}, u32[]{:S(2)}) copy-start(bf16[1,1,1,512,512]{4,3,2,1,0:T(8,128)(2,1)} %param.11) | copy-start | bytes 1572868
  168.0 60.9 %all-to-all-start.1 = ((bf16[1,64,32,512]{3,2,0,1:T(8,128)(2,1)}), bf16[1,64,32,512]{3,2,0,1:T(8,128)(2,1)S(1)}, u32[]{:S(2)}, u32[]{:S(2)}) async-start(bf16[1,64,32,512]{3,2,0,1:T(8,128)(2,1)} %bitcast.62), calls=%async_computation.1 | async-start | bytes 4194304 | tf_op jit(solution)/shard_map/all_to_all | solution.py:92
  178.4 2.8 %copy-start.2 = (f32[1,1,1,512,512]{4,3,2,1,0:T(8,128)S(1)}, f32[1,1,1,512,512]{4,3,2,1,0:T(8,128)}, u32[]{:S(2)}) copy-start(f32[1,1,1,512,512]{4,3,2,1,0:T(8,128)} %param.13) | copy-start | bytes 3145732
  181.2 1.5 copy-start.4
Sparse Core Ops, SparseCore 0:
  10.4 55.6 all-reduce.1
  138.1 29.8 all-gather.2
where the time goes:
time: 240 us; the launch traced here: 239 us
  waiting for transfers between devices  180 us (75%)
  starting transfers between devices  21.3 us (9%)
  between operations  15.6 us (6%)
  matrix products  9.56 us (4%)
  local copies, waits for them, and re-layouts  7.06 us (3%)
  other arithmetic  5.41 us (2%)
    psum x1, waiting for transfers between devices, local(): lax.psum(shard_grad.astype(jnp.float32).astype(jnp.bfloat16), 'rep')  55 us
    all_to_all x1, waiting for transfers between devices, local(): lax.all_to_all(outbound.reshape(send_shape).astype(jnp.bfloat16), 'fsdp',...  50.1 us
    all_to_all x1, waiting for transfers between devices, local(): lax.all_to_all(every_row.reshape(send_shape), 'fsdp', split_axis=1, conca...  44.7 us
    all_gather x1, waiting for transfers between devices, local(): every_row = lax.all_gather(step_blocks[:, None], 'rep', axis=1, tiled=True)  30 us
    all_to_all x1, starting transfers between devices, local(): lax.all_to_all(outbound.reshape(send_shape).astype(jnp.bfloat16), 'fsdp',...  10.8 us
    all_to_all x1, starting transfers between devices, local(): lax.all_to_all(every_row.reshape(send_shape), 'fsdp', split_axis=1, conca...  10.5 us
  transfers between devices with their start and end apart: 4, of which 4 were waited for; matrix products, arithmetic and copies ran while one was open for 3% of the time, Pallas kernels for 0%

commit v1 on v0

v1 whole, which is shorter than its diff:
```python
import functools

import jax
import jax.numpy as jnp
from jax import lax
from jax.experimental import pallas as pl
from jax.experimental.pallas import tpu as pltpu
from jax.sharding import PartitionSpec as P

MESH = pl.DeviceIdType.MESH

stat_decay = 0.9
graft_decay = 0.99
adam_epsilon = 1e-08
graft_epsilon = 1e-06

bf16 = jnp.bfloat16
f32 = jnp.float32


def remote(src, dst, send_sem, recv_sem, where):
    return pltpu.make_async_remote_copy(
        src_ref=src,
        dst_ref=dst,
        send_sem=send_sem,
        recv_sem=recv_sem,
        device_id=where,
        device_id_type=MESH,
    )


def kernel(
    sizes,
    pick_ref,
    owner_ref,
    grads_hbm,
    left_root_hbm,
    right_root_hbm,
    moment_hbm,
    direction_ref,
    g_out_ref,
    grads,
    left_root,
    right_root,
    moment,
    stage,
    mine,
    parts,
    outbox,
    g_land,
    conditioned,
    stepped,
    relay,
    arrived,
    chosen,
    load_sem,
    part_send,
    part_recv,
    out_send,
    out_recv,
    relay_send,
    relay_recv,
    back_send,
    back_recv,
    choice_send,
    choice_recv,
    g_sem,
):
    owners, reps, cols, rows, block, lane, per_row = sizes
    f = lax.axis_index("fsdp")
    y = lax.axis_index("rep")
    home = f // per_row
    place = f % per_row

    loads = [
        pltpu.make_async_copy(grads_hbm, grads, load_sem.at[0]),
        pltpu.make_async_copy(left_root_hbm, left_root, load_sem.at[1]),
        pltpu.make_async_copy(right_root_hbm, right_root, load_sem.at[2]),
        pltpu.make_async_copy(moment_hbm, moment, load_sem.at[3]),
    ]
    for load in loads:
        load.start()

    barrier = pltpu.get_barrier_semaphore()

    def greet(to_f, to_y):
        pl.semaphore_signal(barrier, inc=1, device_id=(to_f, to_y), device_id_type=MESH)

    @pl.loop(1, owners)
    def _(k):
        greet((f + k) % owners, y)

    for d in range(1, reps):
        other = (y + d) % reps

        @pl.loop(0, per_row)
        def _(i):
            greet(per_row * y + i, other)

        @pl.when(home != y)
        def _():
            greet(f, other)

    loads[0].wait()
    for d in range(1, reps):
        peer = (y + d) % reps

        @pl.loop(0, cols)
        def _(c):
            start = pl.multiple_of(c * block + peer * lane, lane)
            stage[d - 1, c] = grads[:, pl.ds(start, lane)]

    @pl.loop(0, cols)
    def _(c):
        start = pl.multiple_of(c * block + y * lane, lane)
        mine[c] = grads[:, pl.ds(start, lane)]

    nothing = jnp.zeros((rows, lane), bf16)
    mine[cols] = nothing
    for d in range(reps - 1):
        parts[d, cols] = nothing

    own_plane = home == y
    plane_and_replicas = owners - 1 + reps - 1
    pl.semaphore_wait(
        barrier, jnp.where(own_plane, plane_and_replicas, plane_and_replicas + owners - 1)
    )

    for d in range(1, reps):
        remote(
            stage.at[d - 1],
            parts.at[d - 1, pl.ds(0, cols)],
            part_send.at[d - 1],
            part_recv.at[d - 1],
            (f, (y + d) % reps),
        ).start()

    for d in range(1, reps):
        remote(
            stage.at[d - 1],
            parts.at[d - 1, pl.ds(0, cols)],
            part_send.at[d - 1],
            part_recv.at[d - 1],
            (f, (y + d) % reps),
        ).wait()

    @pl.loop(0, owners)
    def _(o):
        col = pick_ref[home, o]
        total = mine[col].astype(f32)
        for d in range(reps - 1):
            total = total + parts[d, col].astype(f32)
        outbox[o] = total.astype(bf16)
        target = g_land.at[
            pl.ds(pl.multiple_of(place * rows, rows), rows),
            pl.ds(pl.multiple_of(y * lane, lane), lane),
        ]
        here = own_plane & (o == f)

        @pl.when(jnp.logical_not(here))
        def _():
            remote(outbox.at[o], target, out_send, out_recv, (o, home)).start()

        @pl.when(here)
        def _():
            pltpu.make_async_copy(outbox.at[o], target, out_recv).start()

    for load in loads[1:]:
        load.wait()
    pltpu.make_async_copy(g_land, g_land, out_recv).wait()
    g_copy = pltpu.make_async_copy(g_land, g_out_ref, g_sem)
    g_copy.start()

    half = jnp.dot(left_root[...], g_land[...], preferred_element_type=f32).astype(bf16)
    conditioned[...] = jnp.dot(half, right_root[...], preferred_element_type=f32)
    gradient = g_land[...].astype(f32)
    moment_new = graft_decay * moment[...] + (1.0 - graft_decay) * gradient * gradient
    adam_step = gradient / (jnp.sqrt(moment_new) + adam_epsilon)
    count = float(block * block)
    adam_mean = jnp.sum(adam_step * adam_step) / count
    cond = conditioned[...]
    cond_mean = jnp.sum(cond * cond) / count
    ratio = (adam_mean + graft_epsilon) / (cond_mean + graft_epsilon)
    scale = jnp.sqrt(jnp.full((1, 1), ratio, f32))
    for q in range(reps):
        quarter = conditioned[:, q * lane : (q + 1) * lane]
        stepped[q] = (scale * quarter).astype(bf16)

    for d in range(1, reps):
        peer = (y + d) % reps
        remote(
            stepped.at[peer],
            relay.at[d - 1],
            relay_send.at[d - 1],
            relay_recv.at[d - 1],
            (f, peer),
        ).start()

    def send_back(source, row):
        @pl.loop(0, per_row)
        def _(i):
            piece = source.at[pl.ds(pl.multiple_of(i * rows, rows), rows)]
            there = row * per_row + i
            here = there == f

            @pl.when(jnp.logical_not(here))
            def _():
                remote(piece, arrived.at[f], back_send, back_recv, (there, y)).start()

            @pl.when(here)
            def _():
                pltpu.make_async_copy(piece, arrived.at[f], back_recv).start()

    send_back(stepped.at[y], y)
    for d in (1, 3, 2):
        remote(
            stepped.at[(y + d) % reps],
            relay.at[d - 1],
            relay_send.at[d - 1],
            relay_recv.at[d - 1],
            (f, (y + d) % reps),
        ).wait_recv()
        send_back(relay.at[d - 1], (y + reps - d) % reps)

    pltpu.make_async_copy(arrived, arrived, back_recv).wait()

    @pl.loop(0, cols)
    def _(c):
        chosen[y, c] = arrived[owner_ref[home, c]]

    for d in range(1, reps):
        remote(
            chosen.at[y],
            chosen.at[y],
            choice_send.at[d - 1],
            choice_recv.at[d - 1],
            (f, (y + d) % reps),
        ).start()

    def place_quarter(q):
        @pl.loop(0, cols)
        def _(c):
            start = pl.multiple_of(c * block + q * lane, lane)
            direction_ref[:, pl.ds(start, lane)] = chosen[q, c]

    place_quarter(y)
    for d in (1, 3, 2):
        source = (y + reps - d) % reps
        remote(
            chosen.at[source],
            chosen.at[source],
            choice_send.at[d - 1],
            choice_recv.at[d - 1],
            (f, (y + d) % reps),
        ).wait_recv()
        place_quarter(source)

    for d in range(1, reps):
        remote(
            chosen.at[y],
            chosen.at[y],
            choice_send.at[d - 1],
            choice_recv.at[d - 1],
            (f, (y + d) % reps),
        ).wait_send()
        remote(
            stepped.at[(y + d) % reps],
            relay.at[d - 1],
            relay_send.at[d - 1],
            relay_recv.at[d - 1],
            (f, (y + d) % reps),
        ).wait_send()
    g_copy.wait()
    sent = outbox.at[pl.ds(0, owners - 1)]
    pltpu.make_async_copy(sent, sent, out_send).wait()

    @pl.when(jnp.logical_not(own_plane))
    def _():
        last = outbox.at[owners - 1]
        pltpu.make_async_copy(last, last, out_send).wait()

    gone = arrived.at[pl.ds(0, owners - 1)]
    pltpu.make_async_copy(gone, gone, back_send).wait()


def local(replica_grads, block_owner, left_factor, right_factor, left_root, right_root, moment):
    owners = lax.axis_size("fsdp")
    reps = lax.axis_size("rep")
    rows, width = replica_grads.shape[1:]
    block = left_factor.shape[4]
    cols = width // block
    lane = block // reps
    per_row = block // rows
    sizes = (owners, reps, cols, rows, block, lane, per_row)

    columns = jnp.arange(cols, dtype=jnp.int32)
    match = block_owner[:, :, None] == jnp.arange(owners, dtype=jnp.int32)[None, None, :]
    pick = jnp.min(jnp.where(match, columns[None, :, None], cols), axis=1)

    any_space = pl.BlockSpec(memory_space=pl.ANY)
    direction, g = pl.pallas_call(
        functools.partial(kernel, sizes),
        out_shape=(
            jax.ShapeDtypeStruct((rows, width), bf16),
            jax.ShapeDtypeStruct((block, block), bf16),
        ),
        in_specs=[pl.BlockSpec(memory_space=pltpu.SMEM)] * 2 + [any_space] * 4,
        out_specs=(pl.BlockSpec(memory_space=pltpu.VMEM), any_space),
        scratch_shapes=[
            pltpu.VMEM((rows, width), bf16),
            pltpu.VMEM((block, block), bf16),
            pltpu.VMEM((block, block), bf16),
            pltpu.VMEM((block, block), f32),
            pltpu.VMEM((reps - 1, cols, rows, lane), bf16),
            pltpu.VMEM((cols + 1, rows, lane), bf16),
            pltpu.VMEM((reps - 1, cols + 1, rows, lane), bf16),
            pltpu.VMEM((owners, rows, lane), bf16),
            pltpu.VMEM((block, block), bf16),
            pltpu.VMEM((block, block), f32),
            pltpu.VMEM((reps, block, lane), bf16),
            pltpu.VMEM((reps - 1, block, lane), bf16),
            pltpu.VMEM((owners, rows, lane), bf16),
            pltpu.VMEM((reps, cols, rows, lane), bf16),
            pltpu.SemaphoreType.DMA((4,)),
            pltpu.SemaphoreType.DMA((reps - 1,)),
            pltpu.SemaphoreType.DMA((reps - 1,)),
            pltpu.SemaphoreType.DMA,
            pltpu.SemaphoreType.DMA,
            pltpu.SemaphoreType.DMA((reps - 1,)),
            pltpu.SemaphoreType.DMA((reps - 1,)),
            pltpu.SemaphoreType.DMA,
            pltpu.SemaphoreType.DMA,
            pltpu.SemaphoreType.DMA((reps - 1,)),
            pltpu.SemaphoreType.DMA((reps - 1,)),
            pltpu.SemaphoreType.DMA,
        ],
        compiler_params=pltpu.CompilerParams(
            collective_id=0, has_side_effects=True, vmem_limit_bytes=40 * 1024 * 1024
        ),
    )(
        pick,
        block_owner,
        replica_grads.reshape(rows, width),
        left_root.reshape(block, block),
        right_root.reshape(block, block),
        moment.reshape(block, block),
    )

    def gram(old, contract):
        product = lax.dot_general(
            g, g, (((contract,), (contract,)), ((), ())), preferred_element_type=f32
        )
        return stat_decay * old.reshape(block, block) + (1.0 - stat_decay) * product

    left_new = gram(left_factor, 1)
    right_new = gram(right_factor, 0)
    g_wide = g.astype(f32)
    moment_new = graft_decay * moment.reshape(block, block) + (1.0 - graft_decay) * g_wide * g_wide
    state_shape = left_factor.shape
    return (
        direction,
        left_new.reshape(state_shape),
        right_new.reshape(state_shape),
        moment_new.reshape(state_shape),
    )


def solution(mesh):
    state = P("fsdp", "rep", None, None, None)
    return jax.shard_map(
        local,
        mesh=mesh,
        in_specs=(P("rep", "fsdp", None), P(), state, state, state, state, state),
        out_specs=(P("fsdp", None), state, state, state),
        check_vma=False,
    )
```

time: 240 us -> 98.4 us (0.41)
  waiting for transfers between devices: 180 us -> 0 us
  Pallas kernels: 0 us -> 85.8 us
  starting transfers between devices: 21.3 us -> 0 us
  between operations: 15.6 us -> 0.67 us
  matrix products: 9.56 us -> 2.9 us
  other arithmetic: 5.41 us -> 1.27 us
    all_to_all x2 -> x0, waiting for transfers between devices: 94.8 us -> none  [the longest x1 50.1 us: local(): lax.all_to_all(outbound.reshape(send_shape).astype(jnp.bfloat16), 'fsdp',...]
    pallas_call x0 -> x1, Pallas kernels: none -> 85.8 us  [local(): pl.pallas_call(functools.partial(kernel, sizes), out_shape=(jax.ShapeDtyp...]
    psum x1 -> x0, waiting for transfers between devices: 55 us -> none  [local(): lax.psum(shard_grad.astype(jnp.float32).astype(jnp.bfloat16), 'rep')]
    all_gather x1 -> x0, waiting for transfers between devices: 30 us -> none  [local(): every_row = lax.all_gather(step_blocks[:, None], 'rep', axis=1, tiled=True)]
    all_to_all x2 -> x0, starting transfers between devices: 21.2 us -> none  [the longest x1 10.8 us: local(): lax.all_to_all(outbound.reshape(send_shape).astype(jnp.bfloat16), 'fsdp',...]
    dot_general x5 -> x2, matrix products: 9.56 us -> 2.9 us  [gram(): lax.dot_general(g, g, (((contract,), (contract,)), ((), ())), preferred_e...]
    unnamed x14 -> x16, local copies, waits for them, and re-layouts: 1.91 us -> 7.4 us
    reduce_sum x2 -> x0, other arithmetic: 3 us -> none  [the longest x1 2.21 us: precondition(): jnp.mean(adam_step * adam_step, axis=(1, 2)) + graft_epsilon]
  transfers between devices with their start and end apart: 4 -> 0, of which waited for: 4 -> 0; matrix products, arithmetic and copies ran while one was open for 3% -> 0% of each run, Pallas kernels for 0% -> 0%
where the time goes in v1:
time: 98.4 us; the launch traced here: 98 us
  Pallas kernels  85.8 us (87%)
  local copies, waits for them, and re-layouts  7.4 us (8%)
  matrix products  2.9 us (3%)
  other arithmetic  1.27 us (1%)
    pallas_call x1, Pallas kernels, local(): pl.pallas_call(functools.partial(kernel, sizes), out_shape=(jax.ShapeDtyp...  85.8 us
    unnamed x16, local copies, waits for them, and re-layouts  7.4 us
    dot_general x2, matrix products, gram(): lax.dot_general(g, g, (((contract,), (contract,)), ((), ())), preferred_e...  2.9 us

profile of v1, /device:TPU:32, one launch (start us, length us, event | category | flops | bytes accessed | tf_op | source)
XLA Modules:
  0.0 98.0 jit_solution(17578314102050730374)
XLA Ops:
  0.6 0.8 copy.11
  1.4 0.1 select_reduce_fusion.pick_ref
  1.5 0.0 copy-start
  1.5 1.2 %copy-done = f32[1,1,1,512,512]{4,3,2,1,0:T(8,128)S(1)} copy-done((f32[1,1,1,512,512]{4,3,2,1,0:T(8,128)S(1)}, f32[1,1,1,512,512]{4,3,2,1,0:T(8,128)}, u32[]{:S(2)}) %copy-start) | copy-done | bytes 1048600
  2.8 0.0 copy-start.1
  2.8 1.3 %copy-done.1 = bf16[1,32,18944]{2,1,0:T(8,128)(2,1)S(1)} copy-done((bf16[1,32,18944]{2,1,0:T(8,128)(2,1)S(1)}, bf16[1,32,18944]{2,1,0:T(8,128)(2,1)}, u32[]{:S(2)}) %copy-start.1) | copy-done | bytes 1212440
  4.0 0.0 copy-start.2
  4.0 1.0 %copy-done.2 = bf16[1,1,1,512,512]{4,3,2,1,0:T(8,128)(2,1)S(1)} copy-done((bf16[1,1,1,512,512]{4,3,2,1,0:T(8,128)(2,1)S(1)}, bf16[1,1,1,512,512]{4,3,2,1,0:T(8,128)(2,1)}, u32[]{:S(2)}) %copy-start.2) | copy-done | bytes 524312
  5.1 0.0 copy-start.3
  5.1 1.0 %copy-done.3 = bf16[1,1,1,512,512]{4,3,2,1,0:T(8,128)(2,1)S(1)} copy-done((bf16[1,1,1,512,512]{4,3,2,1,0:T(8,128)(2,1)S(1)}, bf16[1,1,1,512,512]{4,3,2,1,0:T(8,128)(2,1)}, u32[]{:S(2)}) %copy-start.3) | copy-done | bytes 524312
  6.1 0.0 copy-start.4
  6.1 0.7 copy-done.4
  6.8 85.8 %shard_map.102 = (bf16[32,18944]{1,0:T(8,128)(2,1)S(1)}, bf16[512,512]{1,0:T(8,128)(2,1)S(1)}) custom-call(s32[4,64]{1,0:T(4,128)S(1)} %select_reduce_fusion.pick_ref, s32[4,37]{1,0:T(4,128)S(1)} %copy-done.4, bf16[32,18944]{1,0:T(8,128)(2,1)S(1)} %bitcast.20, bf16[512,512]{1,0:T(8,128)(2,1)S(1)} %bitcast.21, bf16[512,512]{1,0:T(8,128)(2,1)S(1)} %bitcast.22, ...), custom_call_target="tpu_custom_call" | custom-call | tf_op jit(solution)/shard_map/pallas_call | solution.py:301
  92.6 0.0 copy-start.5
  92.6 1.2 %fusion.5 = f32[1,1,1,512,512]{4,3,2,1,0:T(8,128)} fusion(bf16[512,512]{1,0:T(8,128)(2,1)S(1)} %get-tuple-element.7, f32[1,1,1,512,512]{4,3,2,1,0:T(8,128)S(1)} %copy-done), kind=kLoop, calls=%fused_computation.8 | loop fusion | flops 1310720 | bytes 2621440 | tf_op jit(solution)/shard_map/reshape | solution.py:364
  93.8 0.3 copy-done.5
  94.1 0.0 copy-start.6
  94.1 1.4 %fusion.1 = f32[1,1,1,512,512]{4,3,2,1,0:T(8,128)} fusion(bf16[512,512]{1,0:T(8,128)(2,1)S(1)} %get-tuple-element.7, f32[1,1,1,512,512]{4,3,2,1,0:T(8,128)S(1)} %copy-done.5), kind=kOutput, calls=%fused_computation.3 | convolution fusion | flops 269221888 | bytes 2621440 | tf_op jit(solution)/shard_map/dot_general | solution.py:350
  95.6 0.0 copy-done.6
  95.6 1.5 %fusion.3 = f32[1,1,1,512,512]{4,3,2,1,0:T(8,128)} fusion(bf16[512,512]{1,0:T(8,128)(2,1)S(1)} %get-tuple-element.7, f32[1,1,1,512,512]{4,3,2,1,0:T(8,128)S(1)} %copy-done.6), kind=kOutput, calls=%fused_computation.6 | convolution fusion | flops 269221888 | bytes 2621440 | tf_op jit(solution)/shard_map/dot_general | solution.py:350
  97.0 1.0 %copy.13 = bf16[32,18944]{1,0:T(8,128)(2,1)} copy(bf16[32,18944]{1,0:T(8,128)(2,1)S(1)} %get-tuple-element.12) | data formatting | bytes 2424832
Async XLA Ops:
  1.5 1.2 %copy-start = (f32[1,1,1,512,512]{4,3,2,1,0:T(8,128)S(1)}, f32[1,1,1,512,512]{4,3,2,1,0:T(8,128)}, u32[]{:S(2)}) copy-start(f32[1,1,1,512,512]{4,3,2,1,0:T(8,128)} %param.13) | copy-start | bytes 3145732
  2.8 1.3 %copy-start.1 = (bf16[1,32,18944]{2,1,0:T(8,128)(2,1)S(1)}, bf16[1,32,18944]{2,1,0:T(8,128)(2,1)}, u32[]{:S(2)}) copy-start(bf16[1,32,18944]{2,1,0:T(8,128)(2,1)} %param.7) | copy-start | bytes 3637252
  4.0 1.0 %copy-start.2 = (bf16[1,1,1,512,512]{4,3,2,1,0:T(8,128)(2,1)S(1)}, bf16[1,1,1,512,512]{4,3,2,1,0:T(8,128)(2,1)}, u32[]{:S(2)}) copy-start(bf16[1,1,1,512,512]{4,3,2,1,0:T(8,128)(2,1)} %param.11) | copy-start | bytes 1572868
  5.1 1.0 %copy-start.3 = (bf16[1,1,1,512,512]{4,3,2,1,0:T(8,128)(2,1)S(1)}, bf16[1,1,1,512,512]{4,3,2,1,0:T(8,128)(2,1)}, u32[]{:S(2)}) copy-start(bf16[1,1,1,512,512]{4,3,2,1,0:T(8,128)(2,1)} %param.12) | copy-start | bytes 1572868
  6.1 0.7 copy-start.4
  92.6 1.5 %copy-start.5 = (f32[1,1,1,512,512]{4,3,2,1,0:T(8,128)S(1)}, f32[1,1,1,512,512]{4,3,2,1,0:T(8,128)}, u32[]{:S(2)}) copy-start(f32[1,1,1,512,512]{4,3,2,1,0:T(8,128)} %param.10) | copy-start | bytes 3145732
  94.1 1.5 %copy-start.6 = (f32[1,1,1,512,512]{4,3,2,1,0:T(8,128)S(1)}, f32[1,1,1,512,512]{4,3,2,1,0:T(8,128)}, u32[]{:S(2)}) copy-start(f32[1,1,1,512,512]{4,3,2,1,0:T(8,128)} %param.9) | copy-start | bytes 3145732

commit v2 on v1

v2 whole, which is shorter than its diff:
```python
import functools

import jax
import jax.numpy as jnp
from jax import lax
from jax.experimental import pallas as pl
from jax.experimental.pallas import tpu as pltpu
from jax.sharding import PartitionSpec as P

MESH = pl.DeviceIdType.MESH

stat_decay = 0.9
graft_decay = 0.99
adam_epsilon = 1e-08
graft_epsilon = 1e-06

bf16 = jnp.bfloat16
f32 = jnp.float32

cores, xs = 2, 4
halves = 2


def remote(src, dst, send_sem, recv_sem, where):
    return pltpu.make_async_remote_copy(
        src_ref=src,
        dst_ref=dst,
        send_sem=send_sem,
        recv_sem=recv_sem,
        device_id=where,
        device_id_type=MESH,
    )


def settle(ref, sem):
    pltpu.make_async_copy(ref, ref, sem).wait()


def greet(sem, to_f, to_y):
    pl.semaphore_signal(sem, inc=1, device_id=(to_f, to_y), device_id_type=MESH)


def kernel(
    sizes,
    owner_hbm,
    grads_hbm,
    left_root_hbm,
    right_root_hbm,
    left_hbm,
    right_hbm,
    moment_hbm,
    direction_ref,
    left_new_ref,
    right_new_ref,
    moment_new_ref,
    owner,
    pick_row,
    pick,
    grads,
    left_root,
    right_root,
    left,
    right,
    moment,
    stage,
    mine,
    parts,
    outbox,
    g_land,
    conditioned,
    stepped,
    relay,
    arrived,
    chosen,
    load_sem,
    pick_sem,
    part_send,
    part_recv,
    out_send,
    out_recv,
    relay_send,
    relay_recv,
    back_send,
    back_recv,
    choice_send,
    choice_recv,
    *round_sems,
):
    owners, reps, cols, rows, block, lane, per_row = sizes
    half_rows = rows // halves
    f = lax.axis_index("fsdp")
    y = lax.axis_index("rep")
    home = f // per_row
    place = f % per_row
    own_plane = home == y

    def replica(d):
        return (y + d + reps) % reps

    loads = [
        pltpu.make_async_copy(source, target, load_sem.at[number])
        for number, (source, target) in enumerate(
            (
                (grads_hbm, grads),
                (owner_hbm, owner),
                (left_root_hbm, left_root),
                (right_root_hbm, right_root),
                (moment_hbm, moment),
                (left_hbm, left),
                (right_hbm, right),
            )
        )
    ]
    for load in loads:
        load.start()

    zs = owners // (cores * xs)
    core, x, z = f % cores, f // cores % xs, f // (cores * xs)

    def at(dz, dx, dcore):
        return (((z + dz + zs) % zs) * xs + (x + dx + xs) % xs) * cores + (core + dcore) % cores

    near = [(f, replica(d)) for d in range(1, reps)]
    near += [(at(1, 0, 0), y), (at(-1, 0, 0), y), (at(0, 1, 0), y), (at(0, -1, 0), y), (at(0, 0, 1), y)]
    rounds = (
        [(at(1, 0, 0), y), (at(-1, 0, 0), y), (at(0, 1, 0), y), (at(0, -1, 0), y)],
        [(at(2, 0, 0), y), (at(-2, 0, 0), y)],
        [(at(0, 1, 0), y), (at(0, 2, 0), y), (at(0, 3, 0), y)],
        [(at(0, 0, 1), y)],
        [(f, replica(d)) for d in range(1, reps)],
    )
    barrier = pltpu.get_barrier_semaphore()
    for where in near:
        greet(barrier, *where)

    def quarter_of(h, q, c):
        start = pl.multiple_of(c * block + q * lane, lane)
        return grads[h * half_rows : (h + 1) * half_rows, pl.ds(start, lane)]

    loads[0].wait()
    for h in range(halves):
        for d in range(1, reps):
            peer = replica(d)

            @pl.loop(0, cols)
            def _(c):
                stage[h, d - 1, c] = quarter_of(h, peer, c)

        @pl.loop(0, cols)
        def _(c):
            mine[h, c] = quarter_of(h, y, c)

        nothing = jnp.zeros((half_rows, lane), bf16)
        mine[h, cols] = nothing
        for d in range(1, reps):
            parts[h][d - 1, cols] = nothing

    loads[1].wait()
    owner_of_lane = lax.broadcasted_iota(jnp.int32, pick_row.shape, 1)
    picked = jnp.full(pick_row.shape, cols, jnp.int32)
    for c in range(cols):
        picked = jnp.where(owner_of_lane == owner[home, c], c, picked)
    pick_row[...] = picked
    pick_copy = pltpu.make_async_copy(pick_row, pick, pick_sem)
    pick_copy.start()
    pick_copy.wait()

    def part_copy(h, d):
        return remote(
            stage.at[h, d - 1],
            parts[h].at[d - 1, pl.ds(0, cols)],
            part_send.at[h, d - 1],
            part_recv.at[h, d - 1],
            (f, replica(d)),
        )

    pl.semaphore_wait(barrier, len(near))
    for h in range(halves):
        for d in (2, 1, 3):
            part_copy(h, d).start()
    for number, peers in enumerate(rounds):
        for where in peers:
            greet(round_sems[number], *where)
        pl.semaphore_wait(round_sems[number], len(peers))

    for h in range(halves):
        for d in (1, 3, 2):
            part_copy(h, d).wait_recv()
        row_start = pl.multiple_of(place * rows + h * half_rows, half_rows)
        target = g_land.at[
            pl.ds(row_start, half_rows), pl.ds(pl.multiple_of(y * lane, lane), lane)
        ]

        @pl.loop(0, owners)
        def _(o):
            col = pick[0, o]
            total = mine[h, col].astype(f32)
            for d in range(reps - 1):
                total = total + parts[h][d, col].astype(f32)
            outbox[h, o] = total.astype(bf16)
            here = own_plane & (o == f)

            @pl.when(jnp.logical_not(here))
            def _():
                remote(
                    outbox.at[h, o], target, out_send.at[h], out_recv.at[h], (o, home)
                ).start()

            @pl.when(here)
            def _():
                pltpu.make_async_copy(outbox.at[h, o], target, out_recv.at[h]).start()

    for load in loads[2:]:
        load.wait()
    for h in range(halves):
        settle(arrived[h], out_recv.at[h])

    half = jnp.dot(left_root[...], g_land[...], preferred_element_type=f32).astype(bf16)
    conditioned[...] = jnp.dot(half, right_root[...], preferred_element_type=f32)
    gradient = g_land[...].astype(f32)
    moment_new = graft_decay * moment[...] + (1.0 - graft_decay) * gradient * gradient
    moment_new_ref[...] = moment_new
    adam_step = gradient / (jnp.sqrt(moment_new) + adam_epsilon)
    count = float(block * block)
    adam_mean = jnp.sum(adam_step * adam_step) / count
    cond = conditioned[...]
    cond_mean = jnp.sum(cond * cond) / count
    ratio = (adam_mean + graft_epsilon) / (cond_mean + graft_epsilon)
    scale = jnp.sqrt(jnp.full((1, 1), ratio, f32))
    for q in range(reps):
        quarter = (scale * conditioned[:, q * lane : (q + 1) * lane]).astype(bf16)
        quarter = quarter.reshape(per_row, halves, half_rows, lane)
        for h in range(halves):
            stepped[q, h] = quarter[:, h]

    def relay_copy(h, d):
        return remote(
            stepped.at[replica(d), h],
            relay.at[h, d - 1],
            relay_send.at[h, d - 1],
            relay_recv.at[h, d - 1],
            (f, replica(d)),
        )

    for h in range(halves):
        for d in (1, 3, 2):
            relay_copy(h, d).start()

    def send_back(h, source, row):
        @pl.loop(0, per_row)
        def _(i):
            there = row * per_row + i
            here = there == f
            target = arrived[h].at[f]

            @pl.when(jnp.logical_not(here))
            def _():
                remote(
                    source.at[i], target, back_send.at[h], back_recv.at[h], (there, y)
                ).start()

            @pl.when(here)
            def _():
                pltpu.make_async_copy(source.at[i], target, back_recv.at[h]).start()

    for h in range(halves):
        send_back(h, stepped.at[y, h], y)
        for d in (1, 3, 2):
            relay_copy(h, d).wait_recv()
            send_back(h, relay.at[h, d - 1], replica(-d))

    def gram(old, contract):
        product = lax.dot_general(
            g_land[...],
            g_land[...],
            (((contract,), (contract,)), ((), ())),
            preferred_element_type=f32,
        )
        return stat_decay * old[...] + (1.0 - stat_decay) * product

    left_new_ref[...] = gram(left, 1)
    right_new_ref[...] = gram(right, 0)

    def choice_copy(h, d, source):
        return remote(
            chosen.at[h, source],
            chosen.at[h, source],
            choice_send.at[h, d - 1],
            choice_recv.at[h, d - 1],
            (f, replica(d)),
        )

    for h in range(halves):
        settle(arrived[h], back_recv.at[h])

        @pl.loop(0, cols)
        def _(c):
            chosen[h, y, c] = arrived[h][owner[home, c]]

        for d in (2, 1, 3):
            choice_copy(h, d, y).start()

    def place_quarter(h, q):
        @pl.loop(0, cols)
        def _(c):
            start = pl.multiple_of(c * block + q * lane, lane)
            direction_ref[h * half_rows : (h + 1) * half_rows, pl.ds(start, lane)] = chosen[h, q, c]

    for h in range(halves):
        place_quarter(h, y)
        for d in (1, 3, 2):
            choice_copy(h, d, replica(-d)).wait_recv()
            place_quarter(h, replica(-d))

    for h in range(halves):
        for d in range(1, reps):
            part_copy(h, d).wait_send()
            relay_copy(h, d).wait_send()
            choice_copy(h, d, y).wait_send()
        settle(outbox.at[h, pl.ds(0, owners - 1)], out_send.at[h])

        @pl.when(jnp.logical_not(own_plane))
        def _():
            settle(outbox.at[h, owners - 1], out_send.at[h])

        settle(arrived[h].at[pl.ds(0, owners - 1)], back_send.at[h])


def local(replica_grads, block_owner, left_factor, right_factor, left_root, right_root, moment):
    owners = lax.axis_size("fsdp")
    reps = lax.axis_size("rep")
    rows, width = replica_grads.shape[1:]
    block = left_factor.shape[4]
    cols = width // block
    lane = block // reps
    per_row = block // rows
    half_rows = rows // halves
    sizes = (owners, reps, cols, rows, block, lane, per_row)

    hbm = pl.BlockSpec(memory_space=pltpu.HBM)
    vmem = pl.BlockSpec(memory_space=pltpu.VMEM)
    square = jax.ShapeDtypeStruct((block, block), f32)
    results = (jax.ShapeDtypeStruct((rows, width), bf16), square, square, square)
    others = reps - 1
    by_half = pltpu.SemaphoreType.DMA((halves,))
    by_peer = pltpu.SemaphoreType.DMA((halves, others))
    flat = [
        array.reshape(block, block)
        for array in (left_root, right_root, left_factor, right_factor, moment)
    ]
    outs = pl.pallas_call(
        functools.partial(kernel, sizes),
        out_shape=results,
        in_specs=[hbm] * 7,
        out_specs=(vmem,) * 4,
        scratch_shapes=[
            pltpu.SMEM(block_owner.shape, jnp.int32),
            pltpu.VMEM((8, 128), jnp.int32),
            pltpu.SMEM((8, 128), jnp.int32),
            pltpu.VMEM((rows, width), bf16),
            pltpu.VMEM((block, block), bf16),
            pltpu.VMEM((block, block), bf16),
            pltpu.VMEM((block, block), f32),
            pltpu.VMEM((block, block), f32),
            pltpu.VMEM((block, block), f32),
            pltpu.VMEM((halves, others, cols, half_rows, lane), bf16),
            pltpu.VMEM((halves, cols + 1, half_rows, lane), bf16),
            [pltpu.VMEM((others, cols + 1, half_rows, lane), bf16)] * halves,
            pltpu.VMEM((halves, owners, half_rows, lane), bf16),
            pltpu.VMEM((block, block), bf16),
            pltpu.VMEM((block, block), f32),
            pltpu.VMEM((reps, halves, per_row, half_rows, lane), bf16),
            pltpu.VMEM((halves, others, per_row, half_rows, lane), bf16),
            [pltpu.VMEM((owners, half_rows, lane), bf16)] * halves,
            pltpu.VMEM((halves, reps, cols, half_rows, lane), bf16),
            pltpu.SemaphoreType.DMA((7,)),
            pltpu.SemaphoreType.DMA,
            by_peer,
            by_peer,
            by_half,
            by_half,
            by_peer,
            by_peer,
            by_half,
            by_half,
            by_peer,
            by_peer,
        ]
        + [pltpu.SemaphoreType.REGULAR] * 5,
        compiler_params=pltpu.CompilerParams(
            collective_id=0, has_side_effects=True, vmem_limit_bytes=24 * 1024 * 1024
        ),
    )(
        *(
            pltpu.with_memory_space_constraint(array, pltpu.HBM)
            for array in (block_owner, replica_grads.reshape(rows, width), *flat)
        )
    )

    direction, left_new, right_new, moment_new = outs
    state_shape = left_factor.shape
    return (
        direction,
        left_new.reshape(state_shape),
        right_new.reshape(state_shape),
        moment_new.reshape(state_shape),
    )


def solution(mesh):
    state = P("fsdp", "rep", None, None, None)
    return jax.shard_map(
        local,
        mesh=mesh,
        in_specs=(P("rep", "fsdp", None), P(), state, state, state, state, state),
        out_specs=(P("fsdp", None), state, state, state),
        check_vma=False,
    )
```

time: 98.4 us -> 74.6 us (0.76)
  the two profiles are of different devices: /device:TPU:32 before, /device:TPU:57 now
where the time goes in v2:
time: 74.6 us; the launch traced here: 74.5 us
  Pallas kernels  70 us (94%)
  local copies, waits for them, and re-layouts  3.93 us (5%)
    pallas_call x1, Pallas kernels, local(): pl.pallas_call(functools.partial(kernel, sizes), out_shape=results, in_sp...  70 us
    unnamed x4, local copies, waits for them, and re-layouts  3.93 us

profile of v2, /device:TPU:57, one launch (start us, length us, event | category | flops | bytes accessed | tf_op | source)
XLA Modules:
  0.0 74.5 jit_solution(6656124399660540653)
XLA Ops:
  0.6 70.0 %shard_map.102 = (bf16[32,18944]{1,0:T(8,128)(2,1)S(1)}, f32[512,512]{1,0:T(8,128)S(1)}, f32[512,512]{1,0:T(8,128)S(1)}, f32[512,512]{1,0:T(8,128)S(1)}) custom-call(s32[4,37]{1,0:T(4,128)} %owner_hbm.1, bf16[32,18944]{1,0:T(8,128)(2,1)} %bitcast.12, bf16[512,512]{1,0:T(8,128)(2,1)} %bitcast.16, bf16[512,512]{1,0:T(8,128)(2,1)} %bitcast.17, ...), custom_call_target="tpu_custom_call" | custom-call | tf_op jit(solution)/shard_map/pallas_call | solution.py:351
  70.6 1.0 %copy.15 = bf16[32,18944]{1,0:T(8,128)(2,1)} copy(bf16[32,18944]{1,0:T(8,128)(2,1)S(1)} %get-tuple-element.16) | data formatting | bytes 2424832
  71.6 1.0 %copy.16 = f32[1,1,1,512,512]{4,3,2,1,0:T(8,128)} copy(f32[1,1,1,512,512]{4,3,2,1,0:T(8,128)S(1)} %bitcast.11) | data formatting | bytes 2097152
  72.6 1.0 %copy.17 = f32[1,1,1,512,512]{4,3,2,1,0:T(8,128)} copy(f32[1,1,1,512,512]{4,3,2,1,0:T(8,128)S(1)} %bitcast.10) | data formatting | bytes 2097152
  73.6 1.0 %copy.18 = f32[1,1,1,512,512]{4,3,2,1,0:T(8,128)} copy(f32[1,1,1,512,512]{4,3,2,1,0:T(8,128)S(1)} %bitcast.9) | data formatting | bytes 2097152

commit v3 on v2

--- a/solution.py
+++ b/solution.py
@@ -19,6 +19,7 @@
 
 cores, xs = 2, 4
 halves = 2
+ways = (1, -1)
 
 
 def remote(src, dst, send_sem, recv_sem, where):
@@ -64,6 +65,7 @@
     moment,
     stage,
     mine,
+    via,
     parts,
     outbox,
     g_land,
@@ -120,15 +122,11 @@
     def at(dz, dx, dcore):
         return (((z + dz + zs) % zs) * xs + (x + dx + xs) % xs) * cores + (core + dcore) % cores
 
-    near = [(f, replica(d)) for d in range(1, reps)]
-    near += [(at(1, 0, 0), y), (at(-1, 0, 0), y), (at(0, 1, 0), y), (at(0, -1, 0), y), (at(0, 0, 1), y)]
-    rounds = (
-        [(at(1, 0, 0), y), (at(-1, 0, 0), y), (at(0, 1, 0), y), (at(0, -1, 0), y)],
-        [(at(2, 0, 0), y), (at(-2, 0, 0), y)],
-        [(at(0, 1, 0), y), (at(0, 2, 0), y), (at(0, 3, 0), y)],
-        [(at(0, 0, 1), y)],
-        [(f, replica(d)) for d in range(1, reps)],
-    )
+    replicas = [(f, replica(d)) for d in range(1, reps)]
+    along_z = [(at(d, 0, 0), y) for d in range(1, zs)]
+    layer = [(at(0, dx, dcore), y) for dx in range(xs) for dcore in range(cores) if dx or dcore]
+    near = replicas + along_z + layer
+    rounds = (along_z, replicas)
     barrier = pltpu.get_barrier_semaphore()
     for where in near:
         greet(barrier, *where)
@@ -152,8 +150,8 @@
 
         nothing = jnp.zeros((half_rows, lane), bf16)
         mine[h, cols] = nothing
-        for d in range(1, reps):
-            parts[h][d - 1, cols] = nothing
+        for d in range(2):
+            parts[h][d, cols] = nothing
 
     loads[1].wait()
     owner_of_lane = lax.broadcasted_iota(jnp.int32, pick_row.shape, 1)
@@ -165,27 +163,54 @@
     pick_copy.start()
     pick_copy.wait()
 
-    def part_copy(h, d):
+    spans = ((0, (cols + 1) // 2), ((cols + 1) // 2, cols))
+
+    def part_copy(h, side, leg):
+        way, (first, last) = ways[side], spans[side]
+        span = pl.ds(first, last - first)
+        source, target, where = (
+            (stage.at[h, 1, span], via.at[h, span], replica(way)),
+            (stage.at[h, -way % reps - 1, span], parts[h].at[1, span], replica(-way)),
+            (stage.at[h, way % reps - 1, span], parts[h].at[0, span], replica(way)),
+        )[leg]
         return remote(
-            stage.at[h, d - 1],
-            parts[h].at[d - 1, pl.ds(0, cols)],
-            part_send.at[h, d - 1],
-            part_recv.at[h, d - 1],
-            (f, replica(d)),
+            source, target, part_send.at[h, side, leg], part_recv.at[h, side, leg], (f, where)
         )
 
+    def send_parts(h, leg):
+        for side in range(2):
+            part_copy(h, side, leg).start()
+
+    def pass_on(h):
+        for side in range(2):
+            part_copy(h, side, 0).wait_recv()
+            slot = ways[side] % reps - 1
+
+            @pl.loop(*spans[side])
+            def _(c):
+                both = stage[h, slot, c].astype(f32) + via[h, c].astype(f32)
+                stage[h, slot, c] = both.astype(bf16)
+
+            part_copy(h, side, 2).start()
+
     pl.semaphore_wait(barrier, len(near))
-    for h in range(halves):
-        for d in (2, 1, 3):
-            part_copy(h, d).start()
-    for number, peers in enumerate(rounds):
-        for where in peers:
-            greet(round_sems[number], *where)
-        pl.semaphore_wait(round_sems[number], len(peers))
-
-    for h in range(halves):
-        for d in (1, 3, 2):
-            part_copy(h, d).wait_recv()
+    send_parts(0, 0)
+    send_parts(1, 0)
+    send_parts(0, 1)
+    for where in rounds[0]:
+        greet(round_sems[0], *where)
+    pass_on(0)
+    send_parts(1, 1)
+    pl.semaphore_wait(round_sems[0], len(rounds[0]))
+    for where in rounds[1]:
+        greet(round_sems[1], *where)
+    pass_on(1)
+    pl.semaphore_wait(round_sems[1], len(rounds[1]))
+
+    for h in range(halves):
+        for leg in (1, 2):
+            for side in range(2):
+                part_copy(h, side, leg).wait_recv()
         row_start = pl.multiple_of(place * rows + h * half_rows, half_rows)
         target = g_land.at[
             pl.ds(row_start, half_rows), pl.ds(pl.multiple_of(y * lane, lane), lane)
@@ -195,7 +220,7 @@
         def _(o):
             col = pick[0, o]
             total = mine[h, col].astype(f32)
-            for d in range(reps - 1):
+            for d in range(2):
                 total = total + parts[h][d, col].astype(f32)
             outbox[h, o] = total.astype(bf16)
             here = own_plane & (o == f)
@@ -236,7 +261,7 @@
     def relay_copy(h, d):
         return remote(
             stepped.at[replica(d), h],
-            relay.at[h, d - 1],
+            relay.at[h, d],
             relay_send.at[h, d - 1],
             relay_recv.at[h, d - 1],
             (f, replica(d)),
@@ -246,28 +271,27 @@
         for d in (1, 3, 2):
             relay_copy(h, d).start()
 
-    def send_back(h, source, row):
-        @pl.loop(0, per_row)
-        def _(i):
-            there = row * per_row + i
+    def send_back(h):
+        @pl.loop(0, owners)
+        def _(there):
+            row = there // per_row
+            source = relay.at[h, (y - row + reps) % reps, there % per_row]
             here = there == f
             target = arrived[h].at[f]
 
             @pl.when(jnp.logical_not(here))
             def _():
-                remote(
-                    source.at[i], target, back_send.at[h], back_recv.at[h], (there, y)
-                ).start()
+                remote(source, target, back_send.at[h], back_recv.at[h], (there, y)).start()
 
             @pl.when(here)
             def _():
-                pltpu.make_async_copy(source.at[i], target, back_recv.at[h]).start()
-
-    for h in range(halves):
-        send_back(h, stepped.at[y, h], y)
+                pltpu.make_async_copy(source, target, back_recv.at[h]).start()
+
+    for h in range(halves):
+        relay[h, 0] = stepped[y, h]
         for d in (1, 3, 2):
             relay_copy(h, d).wait_recv()
-            send_back(h, relay.at[h, d - 1], replica(-d))
+        send_back(h)
 
     def gram(old, contract):
         product = lax.dot_general(
@@ -281,14 +305,17 @@
     left_new_ref[...] = gram(left, 1)
     right_new_ref[...] = gram(right, 0)
 
-    def choice_copy(h, d, source):
-        return remote(
-            chosen.at[h, source],
-            chosen.at[h, source],
-            choice_send.at[h, d - 1],
-            choice_recv.at[h, d - 1],
-            (f, replica(d)),
-        )
+    def choice_copy(h, leg):
+        every = pl.ds(0, cols)
+        spread = [pl.ds(first, last - first) for first, last in spans]
+        source, span, where = (
+            (y, every, replica(1)),
+            (y, every, replica(-1)),
+            (replica(-1), spread[0], replica(1)),
+            (replica(1), spread[1], replica(-1)),
+        )[leg]
+        piece = chosen.at[h, source, span]
+        return remote(piece, piece, choice_send.at[h, leg], choice_recv.at[h, leg], (f, where))
 
     for h in range(halves):
         settle(arrived[h], back_recv.at[h])
@@ -297,8 +324,8 @@
         def _(c):
             chosen[h, y, c] = arrived[h][owner[home, c]]
 
-        for d in (2, 1, 3):
-            choice_copy(h, d, y).start()
+        for leg in (0, 1):
+            choice_copy(h, leg).start()
 
     def place_quarter(h, q):
         @pl.loop(0, cols)
@@ -307,16 +334,24 @@
             direction_ref[h * half_rows : (h + 1) * half_rows, pl.ds(start, lane)] = chosen[h, q, c]
 
     for h in range(halves):
-        place_quarter(h, y)
-        for d in (1, 3, 2):
-            choice_copy(h, d, replica(-d)).wait_recv()
-            place_quarter(h, replica(-d))
+        for leg in (0, 1):
+            choice_copy(h, leg).wait_recv()
+            choice_copy(h, leg + 2).start()
+    for h in range(halves):
+        for d in (0, -1, 1):
+            place_quarter(h, replica(d))
+    for h in range(halves):
+        for leg in (2, 3):
+            choice_copy(h, leg).wait_recv()
+        place_quarter(h, replica(2))
 
     for h in range(halves):
         for d in range(1, reps):
-            part_copy(h, d).wait_send()
+            for side in range(2):
+                part_copy(h, side, d - 1).wait_send()
             relay_copy(h, d).wait_send()
-            choice_copy(h, d, y).wait_send()
+        for leg in range(4):
+            choice_copy(h, leg).wait_send()
         settle(outbox.at[h, pl.ds(0, owners - 1)], out_send.at[h])
 
         @pl.when(jnp.logical_not(own_plane))
@@ -324,6 +359,18 @@
             settle(outbox.at[h, owners - 1], out_send.at[h])
 
         settle(arrived[h].at[pl.ds(0, owners - 1)], back_send.at[h])
+
+
+def finish(*refs):
+    count = len(refs) // 2
+    sem = refs[-1]
+    copies = [
+        pltpu.make_async_copy(refs[i], refs[count + i], sem.at[i]) for i in range(count)
+    ]
+    for copy in copies:
+        copy.start()
+    for copy in copies:
+        copy.wait()
 
 
 def local(replica_grads, block_owner, left_factor, right_factor, left_root, right_root, moment):
@@ -344,6 +391,8 @@
     others = reps - 1
     by_half = pltpu.SemaphoreType.DMA((halves,))
     by_peer = pltpu.SemaphoreType.DMA((halves, others))
+    by_side = pltpu.SemaphoreType.DMA((halves, 2, 3))
+    by_leg = pltpu.SemaphoreType.DMA((halves, 4))
     flat = [
         array.reshape(block, block)
         for array in (left_root, right_root, left_factor, right_factor, moment)
@@ -365,28 +414,29 @@
             pltpu.VMEM((block, block), f32),
             pltpu.VMEM((halves, others, cols, half_rows, lane), bf16),
             pltpu.VMEM((halves, cols + 1, half_rows, lane), bf16),
-            [pltpu.VMEM((others, cols + 1, half_rows, lane), bf16)] * halves,
+            pltpu.VMEM((halves, cols, half_rows, lane), bf16),
+            [pltpu.VMEM((2, cols + 1, half_rows, lane), bf16)] * halves,
             pltpu.VMEM((halves, owners, half_rows, lane), bf16),
             pltpu.VMEM((block, block), bf16),
             pltpu.VMEM((block, block), f32),
             pltpu.VMEM((reps, halves, per_row, half_rows, lane), bf16),
-            pltpu.VMEM((halves, others, per_row, half_rows, lane), bf16),
+            pltpu.VMEM((halves, reps, per_row, half_rows, lane), bf16),
             [pltpu.VMEM((owners, half_rows, lane), bf16)] * halves,
             pltpu.VMEM((halves, reps, cols, half_rows, lane), bf16),
             pltpu.SemaphoreType.DMA((7,)),
             pltpu.SemaphoreType.DMA,
-            by_peer,
-            by_peer,
+            by_side,
+            by_side,
             by_half,
             by_half,
             by_peer,
             by_peer,
             by_half,
             by_half,
-            by_peer,
-            by_peer,
+            by_leg,
+            by_leg,
         ]
-        + [pltpu.SemaphoreType.REGULAR] * 5,
+        + [pltpu.SemaphoreType.REGULAR] * 2,
         compiler_params=pltpu.CompilerParams(
             collective_id=0, has_side_effects=True, vmem_limit_bytes=24 * 1024 * 1024
         ),
@@ -397,7 +447,14 @@
         )
     )
 
-    direction, left_new, right_new, moment_new = outs
+    direction, left_new, right_new, moment_new = pl.pallas_call(
+        finish,
+        out_shape=results,
+        in_specs=[vmem] * 4,
+        out_specs=(hbm,) * 4,
+        scratch_shapes=[pltpu.SemaphoreType.DMA((4,))],
+        compiler_params=pltpu.CompilerParams(vmem_limit_bytes=1024*1024),
+    )(*(pltpu.with_memory_space_constraint(array, pltpu.VMEM) for array in outs))
     state_shape = left_factor.shape
     return (
         direction,

time: 74.6 us -> 68.3 us (0.916)
  the two profiles are of different devices: /device:TPU:57 before, /device:TPU:32 now
where the time goes in v3:
time: 68.3 us; the launch traced here: 67.8 us
  Pallas kernels  67.1 us (98%)
    pallas_call x1, Pallas kernels, local(): pl.pallas_call(functools.partial(kernel, sizes), out_shape=results, in_sp...  65 us
    pallas_call x1, Pallas kernels, local(): pl.pallas_call(finish, out_shape=results, in_specs=[vmem] * 4, out_specs=...  2.1 us

profile of v3, /device:TPU:32, one launch (start us, length us, event | category | flops | bytes accessed | tf_op | source)
XLA Modules:
  0.0 67.8 jit_solution(2823577108854542650)
XLA Ops:
  0.6 65.0 %shard_map.102 = (bf16[32,18944]{1,0:T(8,128)(2,1)S(1)}, f32[512,512]{1,0:T(8,128)S(1)}, f32[512,512]{1,0:T(8,128)S(1)}, f32[512,512]{1,0:T(8,128)S(1)}) custom-call(s32[4,37]{1,0:T(4,128)} %owner_hbm.1, bf16[32,18944]{1,0:T(8,128)(2,1)} %bitcast.9, bf16[512,512]{1,0:T(8,128)(2,1)} %bitcast.13, bf16[512,512]{1,0:T(8,128)(2,1)} %bitcast.14, ...), custom_call_target="tpu_custom_call" | custom-call | tf_op jit(solution)/shard_map/pallas_call | solution.py:400
  65.7 2.1 %shard_map.103 = (bf16[32,18944]{1,0:T(8,128)(2,1)}, f32[512,512]{1,0:T(8,128)}, f32[512,512]{1,0:T(8,128)}, f32[512,512]{1,0:T(8,128)}) custom-call(bf16[32,18944]{1,0:T(8,128)(2,1)S(1)} %get-tuple-element.12.refs_0_, f32[512,512]{1,0:T(8,128)S(1)} %get-tuple-element.13.refs_1_, f32[512,512]{1,0:T(8,128)S(1)} %get-tuple-element.14.refs_2_, ...), custom_call_target="tpu_custom_call" | custom-call | tf_op jit(solution)/shard_map/pallas_call | solution.py:450

commit v4 on v3

--- a/solution.py
+++ b/solution.py
@@ -113,7 +113,7 @@
             )
         )
     ]
-    for load in loads:
+    for load in loads[:2]:
         load.start()
 
     zs = owners // (cores * xs)
@@ -123,45 +123,28 @@
         return (((z + dz + zs) % zs) * xs + (x + dx + xs) % xs) * cores + (core + dcore) % cores
 
     replicas = [(f, replica(d)) for d in range(1, reps)]
-    along_z = [(at(d, 0, 0), y) for d in range(1, zs)]
+    close = [(at(d, 0, 0), y) for d in (1, -1, 2, -2)]
     layer = [(at(0, dx, dcore), y) for dx in range(xs) for dcore in range(cores) if dx or dcore]
-    near = replicas + along_z + layer
-    rounds = (along_z, replicas)
+    near = replicas + close + layer
+    rounds = (close, close[2:], replicas)
     barrier = pltpu.get_barrier_semaphore()
     for where in near:
         greet(barrier, *where)
 
-    def quarter_of(h, q, c):
-        start = pl.multiple_of(c * block + q * lane, lane)
-        return grads[h * half_rows : (h + 1) * half_rows, pl.ds(start, lane)]
+    def set_out(d):
+        for h in range(halves):
+
+            @pl.loop(0, cols, unroll=True)
+            def _(c):
+                start = pl.multiple_of(c * block + replica(d) * lane, lane)
+                piece = grads[h * half_rows : (h + 1) * half_rows, pl.ds(start, lane)]
+                if d:
+                    stage[h, d - 1, c] = piece
+                else:
+                    mine[h, c] = piece
 
     loads[0].wait()
-    for h in range(halves):
-        for d in range(1, reps):
-            peer = replica(d)
-
-            @pl.loop(0, cols)
-            def _(c):
-                stage[h, d - 1, c] = quarter_of(h, peer, c)
-
-        @pl.loop(0, cols)
-        def _(c):
-            mine[h, c] = quarter_of(h, y, c)
-
-        nothing = jnp.zeros((half_rows, lane), bf16)
-        mine[h, cols] = nothing
-        for d in range(2):
-            parts[h][d, cols] = nothing
-
-    loads[1].wait()
-    owner_of_lane = lax.broadcasted_iota(jnp.int32, pick_row.shape, 1)
-    picked = jnp.full(pick_row.shape, cols, jnp.int32)
-    for c in range(cols):
-        picked = jnp.where(owner_of_lane == owner[home, c], c, picked)
-    pick_row[...] = picked
-    pick_copy = pltpu.make_async_copy(pick_row, pick, pick_sem)
-    pick_copy.start()
-    pick_copy.wait()
+    set_out(2)
 
     spans = ((0, (cols + 1) // 2), ((cols + 1) // 2, cols))
 
@@ -186,7 +169,7 @@
             part_copy(h, side, 0).wait_recv()
             slot = ways[side] % reps - 1
 
-            @pl.loop(*spans[side])
+            @pl.loop(*spans[side], unroll=True)
             def _(c):
                 both = stage[h, slot, c].astype(f32) + via[h, c].astype(f32)
                 stage[h, slot, c] = both.astype(bf16)
@@ -196,16 +179,40 @@
     pl.semaphore_wait(barrier, len(near))
     send_parts(0, 0)
     send_parts(1, 0)
+    set_out(1)
+    set_out(3)
     send_parts(0, 1)
     for where in rounds[0]:
         greet(round_sems[0], *where)
-    pass_on(0)
-    send_parts(1, 1)
+    for load in loads[2:]:
+        load.start()
+    set_out(0)
+    for h in range(halves):
+        nothing = jnp.zeros((half_rows, lane), bf16)
+        mine[h, cols] = nothing
+        for d in range(2):
+            parts[h][d, cols] = nothing
+
+    loads[1].wait()
+    owner_of_lane = lax.broadcasted_iota(jnp.int32, pick_row.shape, 1)
+    picked = jnp.full(pick_row.shape, cols, jnp.int32)
+    for c in range(cols):
+        picked = jnp.where(owner_of_lane == owner[home, c], c, picked)
+    pick_row[...] = picked
+    pick_copy = pltpu.make_async_copy(pick_row, pick, pick_sem)
+    pick_copy.start()
+    pick_copy.wait()
+
     pl.semaphore_wait(round_sems[0], len(rounds[0]))
     for where in rounds[1]:
         greet(round_sems[1], *where)
+    pass_on(0)
+    send_parts(1, 1)
+    pl.semaphore_wait(round_sems[1], len(rounds[1]))
+    for where in rounds[2]:
+        greet(round_sems[2], *where)
     pass_on(1)
-    pl.semaphore_wait(round_sems[1], len(rounds[1]))
+    pl.semaphore_wait(round_sems[2], len(rounds[2]))
 
     for h in range(halves):
         for leg in (1, 2):
@@ -258,22 +265,27 @@
         for h in range(halves):
             stepped[q, h] = quarter[:, h]
 
-    def relay_copy(h, d):
+    groups = [(h, j) for h in range(halves) for j in range(2)]
+    group_rows = per_row // 2
+
+    def relay_copy(h, j, d):
+        span = pl.ds(j * group_rows, group_rows)
         return remote(
-            stepped.at[replica(d), h],
-            relay.at[h, d],
-            relay_send.at[h, d - 1],
-            relay_recv.at[h, d - 1],
+            stepped.at[replica(d), h, span],
+            relay.at[h, d, span],
+            relay_send.at[h, j, d - 1],
+            relay_recv.at[h, j, d - 1],
             (f, replica(d)),
         )
 
-    for h in range(halves):
+    for h, j in groups[:2]:
         for d in (1, 3, 2):
-            relay_copy(h, d).start()
-
-    def send_back(h):
-        @pl.loop(0, owners)
-        def _(there):
+            relay_copy(h, j, d).start()
+
+    def send_back(h, j):
+        @pl.loop(0, reps * group_rows)
+        def _(k):
+            there = k // group_rows * per_row + j * group_rows + k % group_rows
             row = there // per_row
             source = relay.at[h, (y - row + reps) % reps, there % per_row]
             here = there == f
@@ -289,9 +301,12 @@
 
     for h in range(halves):
         relay[h, 0] = stepped[y, h]
+    for number, (h, j) in enumerate(groups):
         for d in (1, 3, 2):
-            relay_copy(h, d).wait_recv()
-        send_back(h)
+            relay_copy(h, j, d).wait_recv()
+            if number + 2 < len(groups):
+                relay_copy(*groups[number + 2], d).start()
+        send_back(h, j)
 
     def gram(old, contract):
         product = lax.dot_general(
@@ -306,11 +321,12 @@
     right_new_ref[...] = gram(right, 0)
 
     def choice_copy(h, leg):
-        every = pl.ds(0, cols)
         spread = [pl.ds(first, last - first) for first, last in spans]
         source, span, where = (
-            (y, every, replica(1)),
-            (y, every, replica(-1)),
+            (y, spread[0], replica(1)),
+            (y, spread[1], replica(-1)),
+            (y, spread[1], replica(1)),
+            (y, spread[0], replica(-1)),
             (replica(-1), spread[0], replica(1)),
             (replica(1), spread[1], replica(-1)),
         )[leg]
@@ -320,15 +336,15 @@
     for h in range(halves):
         settle(arrived[h], back_recv.at[h])
 
-        @pl.loop(0, cols)
+        @pl.loop(0, cols, unroll=True)
         def _(c):
             chosen[h, y, c] = arrived[h][owner[home, c]]
 
-        for leg in (0, 1):
+        for leg in range(4):
             choice_copy(h, leg).start()
 
     def place_quarter(h, q):
-        @pl.loop(0, cols)
+        @pl.loop(0, cols, unroll=True)
         def _(c):
             start = pl.multiple_of(c * block + q * lane, lane)
             direction_ref[h * half_rows : (h + 1) * half_rows, pl.ds(start, lane)] = chosen[h, q, c]
@@ -336,12 +352,15 @@
     for h in range(halves):
         for leg in (0, 1):
             choice_copy(h, leg).wait_recv()
-            choice_copy(h, leg + 2).start()
-    for h in range(halves):
-        for d in (0, -1, 1):
+            choice_copy(h, leg + 4).start()
+    for h in range(halves):
+        place_quarter(h, y)
+        for leg in (2, 3):
+            choice_copy(h, leg).wait_recv()
+        for d in (-1, 1):
             place_quarter(h, replica(d))
     for h in range(halves):
-        for leg in (2, 3):
+        for leg in (4, 5):
             choice_copy(h, leg).wait_recv()
         place_quarter(h, replica(2))
 
@@ -349,8 +368,9 @@
         for d in range(1, reps):
             for side in range(2):
                 part_copy(h, side, d - 1).wait_send()
-            relay_copy(h, d).wait_send()
-        for leg in range(4):
+            for j in range(2):
+                relay_copy(h, j, d).wait_send()
+        for leg in range(6):
             choice_copy(h, leg).wait_send()
         settle(outbox.at[h, pl.ds(0, owners - 1)], out_send.at[h])
 
@@ -389,10 +409,10 @@
     square = jax.ShapeDtypeStruct((block, block), f32)
     results = (jax.ShapeDtypeStruct((rows, width), bf16), square, square, square)
     others = reps - 1
+    by_group = pltpu.SemaphoreType.DMA((halves, 2, others))
     by_half = pltpu.SemaphoreType.DMA((halves,))
-    by_peer = pltpu.SemaphoreType.DMA((halves, others))
     by_side = pltpu.SemaphoreType.DMA((halves, 2, 3))
-    by_leg = pltpu.SemaphoreType.DMA((halves, 4))
+    by_leg = pltpu.SemaphoreType.DMA((halves, 6))
     flat = [
         array.reshape(block, block)
         for array in (left_root, right_root, left_factor, right_factor, moment)
@@ -429,14 +449,14 @@
             by_side,
             by_half,
             by_half,
-            by_peer,
-            by_peer,
+            by_group,
+            by_group,
             by_half,
             by_half,
             by_leg,
             by_leg,
         ]
-        + [pltpu.SemaphoreType.REGULAR] * 2,
+        + [pltpu.SemaphoreType.REGULAR] * 3,
         compiler_params=pltpu.CompilerParams(
             collective_id=0, has_side_effects=True, vmem_limit_bytes=24 * 1024 * 1024
         ),

time: 68.3 us -> 65.3 us (0.956)
  Pallas kernels: 67.1 us -> 64.6 us
    pallas_call x1, Pallas kernels: 65 us -> 62.5 us  [local(): pl.pallas_call(functools.partial(kernel, sizes), out_shape=results, in_sp...]
where the time goes in v4:
time: 65.3 us; the launch traced here: 65.2 us
  Pallas kernels  64.6 us (99%)
    pallas_call x1, Pallas kernels, local(): pl.pallas_call(functools.partial(kernel, sizes), out_shape=results, in_sp...  62.5 us
    pallas_call x1, Pallas kernels, local(): pl.pallas_call(finish, out_shape=results, in_specs=[vmem] * 4, out_specs=...  2.1 us

profile of v4, /device:TPU:32, one launch (start us, length us, event | category | flops | bytes accessed | tf_op | source)
XLA Modules:
  0.0 65.2 jit_solution(9096900762744943031)
XLA Ops:
  0.6 62.5 %shard_map.102 = (bf16[32,18944]{1,0:T(8,128)(2,1)S(1)}, f32[512,512]{1,0:T(8,128)S(1)}, f32[512,512]{1,0:T(8,128)S(1)}, f32[512,512]{1,0:T(8,128)S(1)}) custom-call(s32[4,37]{1,0:T(4,128)} %owner_hbm.1, bf16[32,18944]{1,0:T(8,128)(2,1)} %bitcast.9, bf16[512,512]{1,0:T(8,128)(2,1)} %bitcast.13, bf16[512,512]{1,0:T(8,128)(2,1)} %bitcast.14, ...), custom_call_target="tpu_custom_call" | custom-call | tf_op jit(solution)/shard_map/pallas_call | solution.py:420
  63.1 2.1 %shard_map.103 = (bf16[32,18944]{1,0:T(8,128)(2,1)}, f32[512,512]{1,0:T(8,128)}, f32[512,512]{1,0:T(8,128)}, f32[512,512]{1,0:T(8,128)}) custom-call(bf16[32,18944]{1,0:T(8,128)(2,1)S(1)} %get-tuple-element.12.refs_0_, f32[512,512]{1,0:T(8,128)S(1)} %get-tuple-element.13.refs_1_, f32[512,512]{1,0:T(8,128)S(1)} %get-tuple-element.14.refs_2_, ...), custom_call_target="tpu_custom_call" | custom-call | tf_op jit(solution)/shard_map/pallas_call | solution.py:470

commit v5 on v4

--- a/solution.py
+++ b/solution.py
@@ -278,7 +278,7 @@
             (f, replica(d)),
         )
 
-    for h, j in groups[:2]:
+    for h, j in groups[:3]:
         for d in (1, 3, 2):
             relay_copy(h, j, d).start()
 
@@ -304,8 +304,8 @@
     for number, (h, j) in enumerate(groups):
         for d in (1, 3, 2):
             relay_copy(h, j, d).wait_recv()
-            if number + 2 < len(groups):
-                relay_copy(*groups[number + 2], d).start()
+            if number + 3 < len(groups):
+                relay_copy(*groups[number + 3], d).start()
         send_back(h, j)
 
     def gram(old, contract):

time: 65.3 us -> 65.9 us (level); the launches traced: 65.2 us -> 65.1 us
  no operation moved by 1% of the time
where the time goes in v5:
time: 65.9 us; the launch traced here: 65.1 us
  Pallas kernels  64.4 us (98%)
    pallas_call x1, Pallas kernels, local(): pl.pallas_call(functools.partial(kernel, sizes), out_shape=results, in_sp...  62.3 us
    pallas_call x1, Pallas kernels, local(): pl.pallas_call(finish, out_shape=results, in_specs=[vmem] * 4, out_specs=...  2.1 us

profile of v5, /device:TPU:32, one launch (start us, length us, event | category | flops | bytes accessed | tf_op | source)
XLA Modules:
  0.0 65.1 jit_solution(3364629584020311695)
XLA Ops:
  0.6 62.3 %shard_map.102 = (bf16[32,18944]{1,0:T(8,128)(2,1)S(1)}, f32[512,512]{1,0:T(8,128)S(1)}, f32[512,512]{1,0:T(8,128)S(1)}, f32[512,512]{1,0:T(8,128)S(1)}) custom-call(s32[4,37]{1,0:T(4,128)} %owner_hbm.1, bf16[32,18944]{1,0:T(8,128)(2,1)} %bitcast.9, bf16[512,512]{1,0:T(8,128)(2,1)} %bitcast.13, bf16[512,512]{1,0:T(8,128)(2,1)} %bitcast.14, ...), custom_call_target="tpu_custom_call" | custom-call | tf_op jit(solution)/shard_map/pallas_call | solution.py:420
  63.0 2.1 %shard_map.103 = (bf16[32,18944]{1,0:T(8,128)(2,1)}, f32[512,512]{1,0:T(8,128)}, f32[512,512]{1,0:T(8,128)}, f32[512,512]{1,0:T(8,128)}) custom-call(bf16[32,18944]{1,0:T(8,128)(2,1)S(1)} %get-tuple-element.12.refs_0_, f32[512,512]{1,0:T(8,128)S(1)} %get-tuple-element.13.refs_1_, f32[512,512]{1,0:T(8,128)S(1)} %get-tuple-element.14.refs_2_, ...), custom_call_target="tpu_custom_call" | custom-call | tf_op jit(solution)/shard_map/pallas_call | solution.py:470
